TPU v7x, 256 devices: a whole 4x4x8 slice. The times are simulated.
256 devices in a mesh: box: 32 (over y, x, z_hi), coef: 8 (over z_lo, core).
Axes of the slice: x: 4, y: 4, z: 8 (z_hi: 2, z_lo: 4; z = z_hi * 4 + z_lo), core: 2. Of those that a mesh axis runs over, the one named last changes fastest.
Arguments:
- coefficients: bfloat16 [32, 24576, 512], P('box', 'coef'), may hold values from -6 to 6
- interp: bfloat16 [4, 2, 2, 2, 256, 256], replicated, may hold values from -0.1875 to 0.1875
- switch: bfloat16 [32, 2, 256, 256], P('box', None, 'coef'), may hold values from -0.25 to 0.25
- grid_offsets: int32 [32, 24576, 2], P('box', 'coef'), may hold values from 0 to 63
Outputs:
- switched: float32 [32, 24576, 512], P('box', 'coef')
All inputs are finite; a program needn't handle non-finite values.
Results may differ from a plain program's by a relative error of at most 0.0063.
Values may be sent and summed in bfloat16 or wider, within the bound.
A program may use at most 128 MiB of HBM per device.

v0:
```python
import math

import jax
import jax.numpy as jnp
from jax import lax
from jax.sharding import PartitionSpec as P

SIDE = 16


def swapped(shard, axis, distance):
    return lax.ppermute(shard, axis, [(i, i ^ 1 << distance) for i in range(lax.axis_size(axis))])


def block(real_part, imag_part):
    top = jnp.concatenate([real_part, imag_part], axis=1)
    bottom = jnp.concatenate([-imag_part, real_part], axis=1)
    return jnp.concatenate([top, bottom], axis=0)


def rotate(state, offsets, level, rank, side):
    points = jnp.arange(rank, dtype=jnp.int32)
    point_x = points // side
    point_y = points % side
    phase = (level + 1) * (offsets[..., 0:1] * point_x + offsets[..., 1:2] * point_y) % 64
    angle = phase.astype(jnp.float32) * (2.0 * math.pi / 64.0)
    cosine = jnp.cos(angle)
    sine = jnp.sin(angle)
    real_in = state[..., :rank]
    imag_in = state[..., rank:]
    return jnp.concatenate(
        [real_in * cosine - imag_in * sine, real_in * sine + imag_in * cosine], axis=-1
    )


def body(coefficients, interp, switch, grid_offsets):
    rank = interp.shape[-1]
    side = SIDE
    levels = interp.shape[0]
    state = coefficients[0].astype(jnp.float32)
    offsets = grid_offsets[0]
    box_index = lax.axis_index("box")
    for level in range(levels):
        bit = box_index >> level & 1
        matrices = interp[level]
        own_pair = matrices[bit, bit]
        own = block(own_pair[0], own_pair[1])
        rotated = rotate(state, offsets, level, rank, side).astype(jnp.bfloat16)
        cross_pair = matrices[bit, 1 - bit]
        cross = block(cross_pair[0], cross_pair[1])
        partner = swapped(rotated, "box", level)
        state = jnp.dot(rotated, own, preferred_element_type=jnp.float32) + jnp.dot(
            partner, cross, preferred_element_type=jnp.float32
        )
    leaving = state.astype(jnp.bfloat16)
    whole_switch = lax.all_gather(switch, "coef", axis=2, tiled=True)
    matrix = block(whole_switch[0, 0], whole_switch[0, 1])
    switched = jnp.dot(leaving, matrix, preferred_element_type=jnp.float32)
    return switched[None]


def solution(mesh):
    in_specs = (P("box", "coef", None), P(), P("box", None, "coef", None), P("box", "coef", None))
    out_specs = P("box", "coef", None)
    return jax.shard_map(body, mesh=mesh, in_specs=in_specs, out_specs=out_specs, check_vma=False)
```

profile of v0, /device:TPU:33, one launch (start us, length us, event | category | flops | bytes accessed | tf_op | source)
XLA Modules:
  0.0 435.1 jit_solution(7754868511454645353)
XLA Ops:
  0.8 3.2 copy.5
  4.8 13.8 %subtract_convert_fusion.3 = (bf16[3072,256]{0,1:T(8,128)(2,1)S(1)}, bf16[3072,256]{0,1:T(8,128)(2,1)S(1)}) fusion(f32[3072,512]{0,1:T(8,128)S(1)} %bitcast_convert_fusion, s32[256]{0:T(256)S(1)} %get-tuple-element.53, s32[3072]{0:T(1024)S(1)} %bitcast.62, s32[256]{0:T(256)S(1)} %get-tuple-element.54, s32[3072]{0:T(1024)S(1)} %bitcast.58), kind=kLoop, calls=%fused_computation.41 | loop fusion | flops 18874368 | bytes 9463808 | tf_op jit(solution)/shard_map/convert.7
  18.7 1.9 pad_maximum_fusion
  20.6 6.0 %collective-permute-start = (bf16[3072,512]{0,1:T(8,128)(2,1)}, bf16[3072,512]{0,1:T(8,128)(2,1)}, u32[]{:S(2)}, u32[]{:S(2)}) collective-permute-start(bf16[3072,512]{0,1:T(8,128)(2,1)} %pad_maximum_fusion), channel_id=1, source_target_pairs={{0,8},{8,0},{16,24},{24,16},{32,40},{40,32},{48,56},{56,48},{64,72... | collective-permute-start | bytes 9437192 | tf_op jit(solution)/shard_map/ppermute | solution.py:12
  26.6 3.9 fusion.114
  30.6 1.8 fusion.20
  32.4 129.8 %collective-permute-done = bf16[3072,512]{0,1:T(8,128)(2,1)} collective-permute-done((bf16[3072,512]{0,1:T(8,128)(2,1)}, bf16[3072,512]{0,1:T(8,128)(2,1)}, u32[]{:S(2)}, u32[]{:S(2)}) %collective-permute-start) | collective-permute-done | bytes 3145760 | tf_op jit(solution)/shard_map/ppermute | solution.py:12
  162.2 3.7 convolution_add_fusion.2
  166.0 13.9 %subtract_convert_fusion.2 = (bf16[3072,256]{0,1:T(8,128)(2,1)S(1)}, bf16[3072,256]{0,1:T(8,128)(2,1)S(1)}) fusion(f32[3072,512]{0,1:T(8,128)S(1)} %convolution_add_fusion.2, s32[256]{0:T(256)S(1)} %get-tuple-element.53, s32[3072]{0:T(1024)S(1)} %bitcast.63, s32[256]{0:T(256)S(1)} %get-tuple-element.54, s32[3072]{0:T(1024)S(1)} %bitcast.59), kind=kLoop, calls=%fused_computation.39 | loop fusion | flops 19660800 | bytes 9463808 | tf_op jit(solution)/shard_map/convert.5
  179.9 1.9 pad_maximum_fusion.1
  186.9 63.4 %collective-permute-done.1 = bf16[3072,512]{0,1:T(8,128)(2,1)} collective-permute-done((bf16[3072,512]{0,1:T(8,128)(2,1)}, bf16[3072,512]{0,1:T(8,128)(2,1)}, u32[]{:S(2)}, u32[]{:S(2)}) %collective-permute-start.1) | collective-permute-done | bytes 3145760 | tf_op jit(solution)/shard_map/ppermute | solution.py:12
  250.3 3.7 convolution_add_fusion.1
  254.0 13.9 %subtract_convert_fusion.1 = (bf16[3072,256]{0,1:T(8,128)(2,1)S(1)}, bf16[3072,256]{0,1:T(8,128)(2,1)S(1)}) fusion(f32[3072,512]{0,1:T(8,128)S(1)} %convolution_add_fusion.1, s32[256]{0:T(256)S(1)} %get-tuple-element.53, s32[3072]{0:T(1024)S(1)} %bitcast.64, s32[256]{0:T(256)S(1)} %get-tuple-element.54, s32[3072]{0:T(1024)S(1)} %bitcast.60), kind=kLoop, calls=%fused_computation.37 | loop fusion | flops 19660800 | bytes 9463808 | tf_op jit(solution)/shard_map/convert.3
  268.0 1.9 pad_maximum_fusion.2
  269.8 2.7 collective-permute-start.2
  274.6 1.8 fusion.50
  276.4 62.4 %collective-permute-done.2 = bf16[3072,512]{0,1:T(8,128)(2,1)} collective-permute-done((bf16[3072,512]{0,1:T(8,128)(2,1)}, bf16[3072,512]{0,1:T(8,128)(2,1)}, u32[]{:S(2)}, u32[]{:S(2)}) %collective-permute-start.2) | collective-permute-done | bytes 3145760 | tf_op jit(solution)/shard_map/ppermute | solution.py:12
  338.9 3.7 convolution_add_fusion
  342.6 13.9 %subtract_convert_fusion = (bf16[3072,256]{0,1:T(8,128)(2,1)S(1)}, bf16[3072,256]{0,1:T(8,128)(2,1)S(1)}) fusion(f32[3072,512]{0,1:T(8,128)S(1)} %convolution_add_fusion, s32[256]{0:T(256)S(1)} %get-tuple-element.53, s32[3072]{0:T(1024)S(1)} %bitcast.65, s32[256]{0:T(256)S(1)} %get-tuple-element.54, s32[3072]{0:T(1024)S(1)} %bitcast.61), kind=kLoop, calls=%fused_computation.35 | loop fusion | flops 19660800 | bytes 9463808 | tf_op jit(solution)/shard_map/convert.1
  356.6 1.9 pad_maximum_fusion.3
  359.8 15.9 %all_gather.3 = bf16[1,2,256,256]{3,2,1,0:T(8,128)(2,1)S(1)} all-gather(bf16[1,2,32,256]{3,2,1,0:T(8,128)(2,1)S(1)} %copy-done), channel_id=1, replica_groups=mesh['box'=32,'coef'=8] {'coef'}, dimensions={2}, use_global_device_ids=true | all-gather | bytes 294912 | tf_op jit(solution)/shard_map/all_gather | solution.py:56
  379.1 4.5 %fusion.65 = f32[3072,512]{1,0:T(8,128)} fusion(bf16[256,256]{1,0:T(8,128)(2,1)S(1)} %get-tuple-element.36, bf16[256,256]{1,0:T(8,128)(2,1)S(1)} %get-tuple-element.33, bf16[256,256]{1,0:T(8,128)(2,1)S(1)} %get-tuple-element.34, bf16[3072,256]{0,1:T(8,128)(2,1)S(1)} %get-tuple-element.22, bf16[3072,256]{0,1:T(8,128)(2,1)S(1)} %get-tuple-element.21), kind=kOutput, calls=%fused_computation.96 | convolution fusion | flops 1619001344 | bytes 9830400 | tf_op jit(solution)/shard_map/dot_general | solution.py:52
  383.6 41.5 %collective-permute-done.3 = bf16[3072,512]{0,1:T(8,128)(2,1)} collective-permute-done((bf16[3072,512]{0,1:T(8,128)(2,1)}, bf16[3072,512]{0,1:T(8,128)(2,1)}, u32[]{:S(2)}, u32[]{:S(2)}) %collective-permute-start.3) | collective-permute-done | bytes 3145760 | tf_op jit(solution)/shard_map/ppermute | solution.py:12
  425.1 10.0 %convolution_bitcast_fusion = f32[1,3072,512]{2,1,0:T(8,128)} fusion(f32[3072,512]{1,0:T(8,128)} %fusion.65, bf16[3072,512]{0,1:T(8,128)(2,1)} %collective-permute-done.3, bf16[256,256]{1,0:T(8,128)(2,1)S(1)} %get-tuple-element.35, bf16[256,256]{1,0:T(8,128)(2,1)S(1)} %get-tuple-element.5, bf16[256,256]{1,0:T(8,128)(2,1)} %get-tuple-element.6, ...), kind=kOutput, calls=%fused_computation.1 | convolution fusion | flops 3228565504 | bytes 16515072 | tf_op jit(solution)/shard_map/dot_general | solution.py:58
  (18 shorter events, 13.5 us)
Async XLA Ops:
  20.6 141.7 %collective-permute-start = (bf16[3072,512]{0,1:T(8,128)(2,1)}, bf16[3072,512]{0,1:T(8,128)(2,1)}, u32[]{:S(2)}, u32[]{:S(2)}) collective-permute-start(bf16[3072,512]{0,1:T(8,128)(2,1)} %pad_maximum_fusion), channel_id=1, source_target_pairs={{0,8},{8,0},{16,24},{24,16},{32,40},{40,32},{48,56},{56,48},{64,72... | collective-permute-start | bytes 9437192 | tf_op jit(solution)/shard_map/ppermute | solution.py:12
  181.8 68.4 %collective-permute-start.1 = (bf16[3072,512]{0,1:T(8,128)(2,1)}, bf16[3072,512]{0,1:T(8,128)(2,1)}, u32[]{:S(2)}, u32[]{:S(2)}) collective-permute-start(bf16[3072,512]{0,1:T(8,128)(2,1)} %pad_maximum_fusion.1), channel_id=1, source_target_pairs={{0,16},{8,24},{16,0},{24,8},{32,48},{40,56},{48,32},{56,40},{64,80... | collective-permute-start | bytes 9437192 | tf_op jit(solution)/shard_map/ppermute | solution.py:12
  269.8 69.0 %collective-permute-start.2 = (bf16[3072,512]{0,1:T(8,128)(2,1)}, bf16[3072,512]{0,1:T(8,128)(2,1)}, u32[]{:S(2)}, u32[]{:S(2)}) collective-permute-start(bf16[3072,512]{0,1:T(8,128)(2,1)} %pad_maximum_fusion.2), channel_id=1, source_target_pairs={{0,32},{8,40},{16,48},{24,56},{32,0},{40,8},{48,16},{56,24},{64,96... | collective-permute-start | bytes 9437192 | tf_op jit(solution)/shard_map/ppermute | solution.py:12
  356.6 3.2 copy-start
  358.5 66.6 %collective-permute-start.3 = (bf16[3072,512]{0,1:T(8,128)(2,1)}, bf16[3072,512]{0,1:T(8,128)(2,1)}, u32[]{:S(2)}, u32[]{:S(2)}) collective-permute-start(bf16[3072,512]{0,1:T(8,128)(2,1)} %pad_maximum_fusion.3), channel_id=1, source_target_pairs={{0,64},{8,72},{16,80},{24,88},{32,96},{40,104},{48,112},{56,120},{... | collective-permute-start | bytes 9437192 | tf_op jit(solution)/shard_map/ppermute | solution.py:12
where the time goes:
time: 440 us; the launch traced here: 435 us
  waiting for transfers between devices  297 us (68%)
  other arithmetic  67.7 us (15%)
  matrix products  31.3 us (7%)
  blocking collectives  15.9 us (4%)
  local copies, waits for them, and re-layouts  11.7 us (3%)
  starting transfers between devices  11.3 us (3%)
    ppermute x4, waiting for transfers between devices, swapped(): lax.ppermute(shard, axis, [(i, i ^ 1 << distance) for i in range(lax.axis...  297 us
    another operation x4, other arithmetic  55.7 us
    all_gather x1, blocking collectives, body(): whole_switch = lax.all_gather(switch, 'coef', axis=2, tiled=True)  15.9 us
    ppermute x4, starting transfers between devices, swapped(): lax.ppermute(shard, axis, [(i, i ^ 1 << distance) for i in range(lax.axis...  11.3 us
    dot_general x3, matrix products, body(): jnp.dot(partner, cross, preferred_element_type=jnp.float32)  11.2 us
    dot_general x4, matrix products, body(): jnp.dot(rotated, own, preferred_element_type=jnp.float32)  10.1 us
    dot_general x1, matrix products, body(): switched = jnp.dot(leaving, matrix, preferred_element_type=jnp.float32)  9.99 us
  transfers between devices with their start and end apart: 4, of which 4 were waited for; matrix products, arithmetic and copies ran while one was open for 5% of the time, Pallas kernels for 0%

commit v1 on v0

v1 whole, which is shorter than its diff:
```python
import math

import jax
import jax.numpy as jnp
from jax import lax
from jax.experimental import pallas as pl
from jax.experimental.pallas import tpu as pltpu
from jax.sharding import PartitionSpec as P

SIDE = 16
MEMBERS = 16
CHUNK = 32
WINDOW = 256
MESH = pl.DeviceIdType.MESH


def turn(phase):
    share = phase * (1.0 / 64.0)
    share = share - jnp.floor(share + 0.5)
    half = share * math.pi
    square = half * half
    sine = half * (1.0 + square * (-1.0 / 6 + square * (1.0 / 120 + square * (-1.0 / 5040 + square * (
        1.0 / 362880 + square * (-1.0 / 39916800 + square * (1.0 / 6227020800)))))))
    cosine = 1.0 + square * (-0.5 + square * (1.0 / 24 + square * (-1.0 / 720 + square * (
        1.0 / 40320 + square * (-1.0 / 3628800 + square * (1.0 / 479001600))))))
    return 1.0 - 2.0 * sine * sine, 2.0 * sine * cosine


def boxes_with(bit, level):
    return [b for b in range(MEMBERS) if b >> level & 1 == bit]


def middle(
    coef_ref, interp_ref, switch_ref, offsets_ref, home_ref, whole_ref,
    arrived, leaving, weights, windows, columns, cosines, sines, cosine_now, sine_now, rotated,
    in_send, in_recv, out_send, out_recv, off_send, off_recv, sw_send, sw_recv, weight_sem,
):
    box, coef = lax.axis_index("box"), lax.axis_index("coef")
    me, base = box % MEMBERS, box // MEMBERS * MEMBERS
    share = coef_ref.shape[1]
    rank = interp_ref.shape[-1]
    levels = interp_ref.shape[0]
    chunks = share // CHUNK
    parts = lax.axis_size("coef")
    rows = switch_ref.shape[1]

    def member(step):
        return (me + step) % MEMBERS

    barrier = pltpu.get_barrier_semaphore()
    for step in range(1, MEMBERS):
        pl.semaphore_signal(barrier, inc=1, device_id=(base + member(step), coef), device_id_type=MESH)
    for step in range(1, parts):
        pl.semaphore_signal(barrier, inc=1, device_id=(box, (coef + step) % parts), device_id_type=MESH)
    pl.semaphore_wait(barrier, MEMBERS - 1 + parts - 1)

    def window(j):
        return offsets_ref.at[:, pl.ds(pl.multiple_of(128 * (3 * (j // 2) + j % 2), 128), WINDOW)]

    def send(src, dst, send_sem, recv_sem, j):
        return pltpu.make_async_remote_copy(
            src, dst, send_sem, recv_sem, device_id=(base + j, coef), device_id_type=MESH
        )

    for step in range(1, MEMBERS):
        j = member(step)
        send(window(j), windows.at[me], off_send, off_recv, j).start()
    pltpu.make_async_copy(window(me), windows.at[me], off_recv).start()

    def at(c):
        return pl.ds(pl.multiple_of(c * CHUNK, CHUNK), CHUNK)

    def send_in(c, carry):
        for step in range(1, MEMBERS):
            j = member(step)
            send(coef_ref.at[j, at(c)], arrived.at[me, at(c)], in_send, in_recv.at[c], j).start()
        pltpu.make_async_copy(coef_ref.at[me, at(c)], arrived.at[me, at(c)], in_recv.at[c]).start()
        return carry

    lax.fori_loop(0, chunks, send_in, 0)

    def piece(src, owner, step):
        return pltpu.make_async_remote_copy(
            src, whole_ref.at[:, pl.ds(pl.multiple_of(owner * rows, rows), rows)], sw_send, sw_recv,
            device_id=(box, (coef + step) % parts), device_id_type=MESH,
        )

    for step in range(1, parts):
        piece(switch_ref, coef, step).start()
    pltpu.make_async_copy(
        switch_ref, whole_ref.at[:, pl.ds(pl.multiple_of(coef * rows, rows), rows)], sw_recv
    ).start()

    loads = []
    for level in range(levels):
        for bit in range(2):
            for side in range(2):
                pair = interp_ref.at[level, bit, bit if side == 0 else 1 - bit]
                top = 2 * rank * side
                for part, row, column in ((0, 0, 0), (1, 0, rank), (0, rank, rank)):
                    loads.append(pltpu.make_async_copy(
                        pair.at[part],
                        weights.at[level, bit, pl.ds(top + row, rank), pl.ds(column, rank)],
                        weight_sem.at[len(loads)],
                    ))
    for load in loads:
        load.start()
    for load in loads:
        load.wait()

    def negate(i, carry):
        level, bit, side = i // 4, i // 2 % 2, i % 2
        top = 2 * rank * side
        weights[level, bit, pl.ds(pl.multiple_of(top + rank, rank), rank), :rank] = -weights[
            level, bit, pl.ds(pl.multiple_of(top, rank), rank), rank:
        ]
        return carry

    lax.fori_loop(0, 4 * levels, negate, 0)

    pltpu.make_async_copy(windows, windows, off_recv).wait()
    columns[...] = jnp.transpose(
        windows[...].reshape(2 * MEMBERS, WINDOW).astype(jnp.float32), (1, 0)
    )
    points = lax.broadcasted_iota(jnp.int32, (1, rank), 1)
    point_x = (points // SIDE).astype(jnp.float32)
    point_y = (points % SIDE).astype(jnp.float32)
    skip = 64 * (me % 2)

    def compute(c, carry):
        pair = columns[pl.ds(pl.multiple_of(skip + c * CHUNK, CHUNK), CHUNK), :]
        for b in range(MEMBERS):
            phase = pair[:, 2 * b:2 * b + 1] * point_x + pair[:, 2 * b + 1:2 * b + 2] * point_y
            cosine, sine = turn(phase)
            cosines[b] = cosine
            sines[b] = sine

        pltpu.make_async_copy(arrived.at[:, at(c)], arrived.at[:, at(c)], in_recv.at[c]).wait()

        for b in range(MEMBERS):
            state = arrived[b, at(c), :].astype(jnp.float32)
            real, imag = state[:, :rank], state[:, rank:]
            cosine, sine = cosines[b], sines[b]
            rotated[0, b, :, :rank] = (real * cosine - imag * sine).astype(jnp.bfloat16)
            rotated[0, b, :, rank:] = (real * sine + imag * cosine).astype(jnp.bfloat16)

        for level in range(levels):
            now, later = level % 2, 1 - level % 2
            for bit in range(2):
                own = jnp.concatenate([rotated[now, b] for b in boxes_with(bit, level)], axis=0)
                cross = jnp.concatenate(
                    [rotated[now, b ^ 1 << level] for b in boxes_with(bit, level)], axis=0
                )
                state = jnp.dot(
                    jnp.concatenate([own, cross], axis=1), weights[level, bit],
                    preferred_element_type=jnp.float32,
                )
                for k, b in enumerate(boxes_with(bit, level)):
                    mine = state[k * CHUNK:(k + 1) * CHUNK]
                    if level == levels - 1:
                        leaving[b, at(c), :] = mine.astype(jnp.bfloat16)
                        continue
                    cosine, sine = cosines[b], sines[b]
                    before_c = cosine if level == 0 else cosine_now[b]
                    before_s = sine if level == 0 else sine_now[b]
                    next_c = before_c * cosine - before_s * sine
                    next_s = before_c * sine + before_s * cosine
                    if level < levels - 2:
                        cosine_now[b] = next_c
                        sine_now[b] = next_s
                    real, imag = mine[:, :rank], mine[:, rank:]
                    rotated[later, b, :, :rank] = (real * next_c - imag * next_s).astype(jnp.bfloat16)
                    rotated[later, b, :, rank:] = (real * next_s + imag * next_c).astype(jnp.bfloat16)

        for step in range(1, MEMBERS):
            j = member(step)
            send(leaving.at[j, at(c)], home_ref.at[me, at(c)], out_send, out_recv, j).start()
        pltpu.make_async_copy(leaving.at[me, at(c)], home_ref.at[me, at(c)], out_recv).start()
        return carry

    lax.fori_loop(0, chunks, compute, 0)

    others = pl.ds(0, MEMBERS - 1)
    send(coef_ref.at[others], arrived.at[others], in_send, out_recv, member(1)).wait_send()
    send(leaving.at[others], home_ref.at[others], out_send, out_recv, member(1)).wait_send()
    send(windows.at[others], windows.at[others], off_send, out_recv, member(1)).wait_send()
    sent = whole_ref.at[:, pl.ds(0, rows * (parts - 1))]
    send(sent, sent, sw_send, out_recv, member(1)).wait_send()
    pltpu.make_async_copy(whole_ref, whole_ref, sw_recv).wait()
    pltpu.make_async_copy(home_ref, home_ref, out_recv).wait()


def last(leaving_ref, switch_ref, out_ref, matrix):
    rank = switch_ref.shape[-1]

    @pl.when(pl.program_id(0) == 0)
    def _():
        matrix[:rank, :rank] = switch_ref[0]
        matrix[:rank, rank:] = switch_ref[1]
        matrix[rank:, :rank] = -switch_ref[1]
        matrix[rank:, rank:] = switch_ref[0]

    out_ref[...] = jnp.dot(leaving_ref[...], matrix[...], preferred_element_type=jnp.float32)


def body(coefficients, interp, switch, grid_offsets):
    _, rows, width = coefficients.shape
    rank = interp.shape[-1]
    levels = interp.shape[0]
    share = rows // MEMBERS
    chunks = share // CHUNK
    bf16, f32 = jnp.bfloat16, jnp.float32
    anywhere = pl.BlockSpec(memory_space=pl.ANY)
    dma = pltpu.SemaphoreType.DMA
    home, whole = pl.pallas_call(
        middle,
        out_shape=(
            jax.ShapeDtypeStruct((MEMBERS, share, width), bf16),
            jax.ShapeDtypeStruct((2, rank, rank), bf16),
        ),
        in_specs=[anywhere] * 4,
        out_specs=(anywhere, anywhere),
        scratch_shapes=[
            pltpu.VMEM((MEMBERS, share, width), bf16),
            pltpu.VMEM((MEMBERS, share, width), bf16),
            pltpu.VMEM((levels, 2, 2 * width, width), bf16),
            pltpu.VMEM((MEMBERS, 2, WINDOW), jnp.int32),
            pltpu.VMEM((WINDOW, 2 * MEMBERS), f32),
            pltpu.VMEM((MEMBERS, CHUNK, rank), f32),
            pltpu.VMEM((MEMBERS, CHUNK, rank), f32),
            pltpu.VMEM((MEMBERS, CHUNK, rank), f32),
            pltpu.VMEM((MEMBERS, CHUNK, rank), f32),
            pltpu.VMEM((2, MEMBERS, CHUNK, width), bf16),
            dma, dma((chunks,)), dma, dma, dma, dma, dma, dma, dma((12 * levels,)),
        ],
        compiler_params=pltpu.CompilerParams(
            collective_id=0, has_side_effects=True, vmem_limit_bytes=48 << 20
        ),
        name="middle",
    )(coefficients.reshape(MEMBERS, share, width), interp, switch[0], jnp.swapaxes(grid_offsets[0], 0, 1))
    tile = 512
    switched = pl.pallas_call(
        last,
        grid=(rows // tile,),
        out_shape=jax.ShapeDtypeStruct((rows, width), f32),
        in_specs=[
            pl.BlockSpec((tile, width), lambda i: (i, 0)),
            pl.BlockSpec((2, rank, rank), lambda i: (0, 0, 0)),
        ],
        out_specs=pl.BlockSpec((tile, width), lambda i: (i, 0)),
        scratch_shapes=[pltpu.VMEM((width, width), bf16)],
        compiler_params=pltpu.CompilerParams(vmem_limit_bytes=32 << 20),
        name="last",
    )(home.reshape(rows, width), whole)
    return switched[None]


def solution(mesh):
    in_specs = (P("box", "coef", None), P(), P("box", None, "coef", None), P("box", "coef", None))
    out_specs = P("box", "coef", None)
    return jax.shard_map(body, mesh=mesh, in_specs=in_specs, out_specs=out_specs, check_vma=False)
```

time: 440 us -> 160 us (0.36)
  waiting for transfers between devices: 297 us -> 0 us
  Pallas kernels: 0 us -> 158 us
  other arithmetic: 67.7 us -> 0 us
  matrix products: 31.3 us -> 0 us
  blocking collectives: 15.9 us -> 0 us
  starting transfers between devices: 11.3 us -> 0 us
  local copies, waits for them, and re-layouts: 11.7 us -> 1.49 us
    ppermute x4 -> x0, waiting for transfers between devices: 297 us -> none  [swapped(): lax.ppermute(shard, axis, [(i, i ^ 1 << distance) for i in range(lax.axis...]
    pallas_call x0 -> x2, Pallas kernels: none -> 158 us  [the longest x1 153 us: body(): pl.pallas_call(middle, out_shape=(jax.ShapeDtypeStruct((MEMBERS, share, w...]
    another operation x4 -> x0, other arithmetic: 55.7 us -> none
    dot_general x8 -> x0, matrix products: 31.3 us -> none  [the longest x3 11.2 us: body(): jnp.dot(partner, cross, preferred_element_type=jnp.float32)]
    all_gather x1 -> x0, blocking collectives: 15.9 us -> none  [body(): whole_switch = lax.all_gather(switch, 'coef', axis=2, tiled=True)]
    ppermute x4 -> x0, starting transfers between devices: 11.3 us -> none  [swapped(): lax.ppermute(shard, axis, [(i, i ^ 1 << distance) for i in range(lax.axis...]
    concatenate x4 -> x0, other arithmetic: 7.47 us -> none  [rotate(): jnp.concatenate([real_in * cosine - imag_in * sine, real_in * sine + imag...]
    slice x2 -> x0, local copies, waits for them, and re-layouts: 4.77 us -> none  [the longest x1 3.93 us: body(): matrices = interp[level]]
  transfers between devices with their start and end apart: 4 -> 0, of which waited for: 4 -> 0; matrix products, arithmetic and copies ran while one was open for 5% -> 0% of each run, Pallas kernels for 0% -> 0%
where the time goes in v1:
time: 160 us; the launch traced here: 159 us
  Pallas kernels  158 us (99%)
    pallas_call x1, Pallas kernels, body(): pl.pallas_call(middle, out_shape=(jax.ShapeDtypeStruct((MEMBERS, share, w...  153 us
    pallas_call x1, Pallas kernels, body(): pl.pallas_call(last, grid=(rows // tile,), out_shape=jax.ShapeDtypeStruct...  4.75 us

profile of v1, /device:TPU:33, one launch (start us, length us, event | category | flops | bytes accessed | tf_op | source)
XLA Modules:
  0.0 159.1 jit_solution(9402830763113562999)
XLA Ops:
  0.0 0.0 copy-start
  0.0 0.8 copy-done
  0.8 0.0 copy-start.1
  0.8 0.7 copy-done.1
  1.5 152.9 %middle.1 = (bf16[16,192,512]{2,1,0:T(8,128)(2,1)S(1)}, bf16[2,256,256]{2,1,0:T(8,128)(2,1)S(1)}) custom-call(bf16[16,192,512]{2,1,0:T(8,128)(2,1)} %bitcast.10, bf16[4,2,2,2,256,256]{5,4,3,2,1,0:T(8,128)(2,1)} %interp_ref.1, bf16[2,32,256]{2,1,0:T(8,128)(2,1)S(1)} %bitcast.8, s32[2,3072]{1,0:T(2,128)S(1)} %bitcast.9), custom_call_target="tpu_custom_call" | custom-call | tf_op jit(solution)/shard_map/middle/pallas_call | solution.py:215
  154.4 4.7 %last.1 = f32[3072,512]{1,0:T(8,128)} custom-call(bf16[3072,512]{1,0:T(8,128)(2,1)S(1)} %bitcast.7, bf16[2,256,256]{2,1,0:T(8,128)(2,1)S(1)} %get-tuple-element.8.switch_ref), custom_call_target="tpu_custom_call" | custom-call | tf_op jit(solution)/shard_map/last/pallas_call | solution.py:242
Async XLA Ops:
  0.0 0.8 copy-start
  0.8 0.7 copy-start.1

commit v2 on v1

--- a/solution.py
+++ b/solution.py
@@ -9,9 +9,12 @@
 
 SIDE = 16
 MEMBERS = 16
-CHUNK = 32
+CHUNK = 64
 WINDOW = 256
 MESH = pl.DeviceIdType.MESH
+STEPS = [(0, 0, 0)] + [
+    (y, x, z) for x, y in ((0, 0), (1, 0), (2, 0), (3, 0), (0, 1), (1, 1), (2, 1), (3, 1)) for z in (1, 0) if x + y + z
+]
 
 
 def turn(phase):
@@ -31,12 +34,14 @@
 
 
 def middle(
-    coef_ref, interp_ref, switch_ref, offsets_ref, home_ref, whole_ref,
-    arrived, leaving, weights, windows, columns, cosines, sines, cosine_now, sine_now, rotated,
-    in_send, in_recv, out_send, out_recv, off_send, off_recv, sw_send, sw_recv, weight_sem,
+    coef_ref, interp_ref, switch_ref, offsets_ref, out_ref,
+    arrived, leaving, home, weights, whole, matrix, windows, columns,
+    cosines, sines, cosine_now, sine_now, rotated,
+    in_send, in_recv, out_send, out_recv, off_send, off_recv, sw_send, sw_recv, sw_other, weight_sem,
 ):
     box, coef = lax.axis_index("box"), lax.axis_index("coef")
     me, base = box % MEMBERS, box // MEMBERS * MEMBERS
+    me_y, me_x, me_z = me // 8, me // 2 % 4, me % 2
     share = coef_ref.shape[1]
     rank = interp_ref.shape[-1]
     levels = interp_ref.shape[0]
@@ -45,14 +50,17 @@
     rows = switch_ref.shape[1]
 
     def member(step):
-        return (me + step) % MEMBERS
+        y, x, z = STEPS[step]
+        return (me_y + y) % 2 * 8 + (me_x + x) % 4 * 2 + (me_z + z) % 2
 
     barrier = pltpu.get_barrier_semaphore()
     for step in range(1, MEMBERS):
         pl.semaphore_signal(barrier, inc=1, device_id=(base + member(step), coef), device_id_type=MESH)
-    for step in range(1, parts):
+    other_core = coef + 1 - 2 * (coef % 2)
+    pl.semaphore_signal(barrier, inc=1, device_id=(box, other_core), device_id_type=MESH)
+    for step in range(2, parts, 2):
         pl.semaphore_signal(barrier, inc=1, device_id=(box, (coef + step) % parts), device_id_type=MESH)
-    pl.semaphore_wait(barrier, MEMBERS - 1 + parts - 1)
+    pl.semaphore_wait(barrier, MEMBERS - 1 + parts // 2)
 
     def window(j):
         return offsets_ref.at[:, pl.ds(pl.multiple_of(128 * (3 * (j // 2) + j % 2), 128), WINDOW)]
@@ -62,13 +70,20 @@
             src, dst, send_sem, recv_sem, device_id=(base + j, coef), device_id_type=MESH
         )
 
-    for step in range(1, MEMBERS):
-        j = member(step)
-        send(window(j), windows.at[me], off_send, off_recv, j).start()
-    pltpu.make_async_copy(window(me), windows.at[me], off_recv).start()
-
     def at(c):
         return pl.ds(pl.multiple_of(c * CHUNK, CHUNK), CHUNK)
+
+    def rows_of(owner):
+        return whole.at[:, pl.ds(pl.multiple_of(owner * rows, rows), rows)]
+
+    def piece(src, owner, recv_sem, target):
+        return pltpu.make_async_remote_copy(
+            src, rows_of(owner), sw_send, recv_sem, device_id=(box, target), device_id_type=MESH
+        )
+
+    for step in range(2, parts, 2):
+        piece(switch_ref, coef, sw_recv, (coef + step) % parts).start()
+    pltpu.make_async_copy(switch_ref, rows_of(coef), sw_recv).start()
 
     def send_in(c, carry):
         for step in range(1, MEMBERS):
@@ -77,19 +92,12 @@
         pltpu.make_async_copy(coef_ref.at[me, at(c)], arrived.at[me, at(c)], in_recv.at[c]).start()
         return carry
 
-    lax.fori_loop(0, chunks, send_in, 0)
-
-    def piece(src, owner, step):
-        return pltpu.make_async_remote_copy(
-            src, whole_ref.at[:, pl.ds(pl.multiple_of(owner * rows, rows), rows)], sw_send, sw_recv,
-            device_id=(box, (coef + step) % parts), device_id_type=MESH,
-        )
-
-    for step in range(1, parts):
-        piece(switch_ref, coef, step).start()
-    pltpu.make_async_copy(
-        switch_ref, whole_ref.at[:, pl.ds(pl.multiple_of(coef * rows, rows), rows)], sw_recv
-    ).start()
+    send_in(0, 0)
+    for step in range(1, MEMBERS):
+        j = member(step)
+        send(window(j), windows.at[me], off_send, off_recv, j).start()
+    pltpu.make_async_copy(window(me), windows.at[me], off_recv).start()
+    lax.fori_loop(1, chunks, send_in, 0)
 
     loads = []
     for level in range(levels):
@@ -174,33 +182,38 @@
 
         for step in range(1, MEMBERS):
             j = member(step)
-            send(leaving.at[j, at(c)], home_ref.at[me, at(c)], out_send, out_recv, j).start()
-        pltpu.make_async_copy(leaving.at[me, at(c)], home_ref.at[me, at(c)], out_recv).start()
+            send(leaving.at[j, at(c)], home.at[me, at(c)], out_send, out_recv.at[c], j).start()
+        pltpu.make_async_copy(leaving.at[me, at(c)], home.at[me, at(c)], out_recv.at[c]).start()
         return carry
 
     lax.fori_loop(0, chunks, compute, 0)
 
+    half = whole.at[:, pl.ds(0, rows * (parts // 2))]
+    pltpu.make_async_copy(half, half, sw_recv).wait()
+    for step in range(0, parts, 2):
+        owner = (coef + step) % parts
+        piece(rows_of(owner), owner, sw_other, other_core).start()
+    pltpu.make_async_copy(half, half, sw_other).wait()
+    matrix[:rank, :rank] = whole[0]
+    matrix[:rank, rank:] = whole[1]
+    matrix[rank:, :rank] = -whole[1]
+    matrix[rank:, rank:] = whole[0]
+
+    def finish(c, carry):
+        pltpu.make_async_copy(home.at[:, at(c)], home.at[:, at(c)], out_recv.at[c]).wait()
+        state = home[:, at(c), :].reshape(MEMBERS * CHUNK, 2 * rank)
+        switched = jnp.dot(state, matrix[...], preferred_element_type=jnp.float32)
+        out_ref[:, at(c), :] = switched.reshape(MEMBERS, CHUNK, 2 * rank)
+        return carry
+
+    lax.fori_loop(0, chunks, finish, 0)
+
     others = pl.ds(0, MEMBERS - 1)
-    send(coef_ref.at[others], arrived.at[others], in_send, out_recv, member(1)).wait_send()
-    send(leaving.at[others], home_ref.at[others], out_send, out_recv, member(1)).wait_send()
-    send(windows.at[others], windows.at[others], off_send, out_recv, member(1)).wait_send()
-    sent = whole_ref.at[:, pl.ds(0, rows * (parts - 1))]
-    send(sent, sent, sw_send, out_recv, member(1)).wait_send()
-    pltpu.make_async_copy(whole_ref, whole_ref, sw_recv).wait()
-    pltpu.make_async_copy(home_ref, home_ref, out_recv).wait()
-
-
-def last(leaving_ref, switch_ref, out_ref, matrix):
-    rank = switch_ref.shape[-1]
-
-    @pl.when(pl.program_id(0) == 0)
-    def _():
-        matrix[:rank, :rank] = switch_ref[0]
-        matrix[:rank, rank:] = switch_ref[1]
-        matrix[rank:, :rank] = -switch_ref[1]
-        matrix[rank:, rank:] = switch_ref[0]
-
-    out_ref[...] = jnp.dot(leaving_ref[...], matrix[...], preferred_element_type=jnp.float32)
+    send(coef_ref.at[others], arrived.at[others], in_send, off_recv, member(1)).wait_send()
+    send(leaving.at[others], home.at[others], out_send, off_recv, member(1)).wait_send()
+    send(windows.at[others], windows.at[others], off_send, off_recv, member(1)).wait_send()
+    sent = whole.at[:, pl.ds(0, rows * (parts - 1))]
+    send(sent, sent, sw_send, off_recv, member(1)).wait_send()
 
 
 def body(coefficients, interp, switch, grid_offsets):
@@ -210,20 +223,22 @@
     share = rows // MEMBERS
     chunks = share // CHUNK
     bf16, f32 = jnp.bfloat16, jnp.float32
-    anywhere = pl.BlockSpec(memory_space=pl.ANY)
     dma = pltpu.SemaphoreType.DMA
-    home, whole = pl.pallas_call(
+    operands = (
+        coefficients.reshape(MEMBERS, share, width), interp, switch[0], jnp.swapaxes(grid_offsets[0], 0, 1)
+    )
+    switched = pl.pallas_call(
         middle,
-        out_shape=(
-            jax.ShapeDtypeStruct((MEMBERS, share, width), bf16),
-            jax.ShapeDtypeStruct((2, rank, rank), bf16),
-        ),
-        in_specs=[anywhere] * 4,
-        out_specs=(anywhere, anywhere),
+        out_shape=pltpu.VMEM((MEMBERS, share, width), f32),
+        in_specs=[pl.BlockSpec(memory_space=pl.ANY)] * 4,
+        out_specs=pl.BlockSpec(memory_space=pltpu.VMEM),
         scratch_shapes=[
             pltpu.VMEM((MEMBERS, share, width), bf16),
             pltpu.VMEM((MEMBERS, share, width), bf16),
+            pltpu.VMEM((MEMBERS, share, width), bf16),
             pltpu.VMEM((levels, 2, 2 * width, width), bf16),
+            pltpu.VMEM((2, rank, rank), bf16),
+            pltpu.VMEM((width, width), bf16),
             pltpu.VMEM((MEMBERS, 2, WINDOW), jnp.int32),
             pltpu.VMEM((WINDOW, 2 * MEMBERS), f32),
             pltpu.VMEM((MEMBERS, CHUNK, rank), f32),
@@ -231,28 +246,14 @@
             pltpu.VMEM((MEMBERS, CHUNK, rank), f32),
             pltpu.VMEM((MEMBERS, CHUNK, rank), f32),
             pltpu.VMEM((2, MEMBERS, CHUNK, width), bf16),
-            dma, dma((chunks,)), dma, dma, dma, dma, dma, dma, dma((12 * levels,)),
+            dma, dma((chunks,)), dma, dma((chunks,)), dma, dma, dma, dma, dma, dma((12 * levels,)),
         ],
         compiler_params=pltpu.CompilerParams(
             collective_id=0, has_side_effects=True, vmem_limit_bytes=48 << 20
         ),
         name="middle",
-    )(coefficients.reshape(MEMBERS, share, width), interp, switch[0], jnp.swapaxes(grid_offsets[0], 0, 1))
-    tile = 512
-    switched = pl.pallas_call(
-        last,
-        grid=(rows // tile,),
-        out_shape=jax.ShapeDtypeStruct((rows, width), f32),
-        in_specs=[
-            pl.BlockSpec((tile, width), lambda i: (i, 0)),
-            pl.BlockSpec((2, rank, rank), lambda i: (0, 0, 0)),
-        ],
-        out_specs=pl.BlockSpec((tile, width), lambda i: (i, 0)),
-        scratch_shapes=[pltpu.VMEM((width, width), bf16)],
-        compiler_params=pltpu.CompilerParams(vmem_limit_bytes=32 << 20),
-        name="last",
-    )(home.reshape(rows, width), whole)
-    return switched[None]
+    )(*[pltpu.with_memory_space_constraint(operand, pltpu.HBM) for operand in operands])
+    return switched.reshape(1, rows, width)
 
 
 def solution(mesh):

time: 160 us -> 157 us (0.981)
  Pallas kernels: 158 us -> 154 us
    pallas_call x2 -> x1, Pallas kernels: 158 us -> 154 us  [body(): pl.pallas_call(middle, out_shape=pltpu.VMEM((MEMBERS, share, width), f32)...]
where the time goes in v2:
time: 157 us
  Pallas kernels  154 us (98%)
  local copies, waits for them, and re-layouts  2.71 us (2%)
    pallas_call x1, Pallas kernels, body(): pl.pallas_call(middle, out_shape=pltpu.VMEM((MEMBERS, share, width), f32)...  154 us

profile of v2, /device:TPU:33, one launch (start us, length us, event | category | flops | bytes accessed | tf_op | source)
XLA Modules:
  0.0 156.7 jit_solution(8624262889241817045)
XLA Ops:
  0.0 153.9 %middle.1 = f32[16,192,512]{2,1,0:T(8,128)S(1)} custom-call(bf16[16,192,512]{2,1,0:T(8,128)(2,1)} %bitcast.7, bf16[4,2,2,2,256,256]{5,4,3,2,1,0:T(8,128)(2,1)} %interp_ref.1, bf16[2,32,256]{2,1,0:T(8,128)(2,1)} %bitcast.8, s32[2,3072]{1,0:T(2,128)} %bitcast.9), custom_call_target="tpu_custom_call" | custom-call | tf_op jit(solution)/shard_map/middle/pallas_call | solution.py:230
  153.9 2.7 %copy.6 = f32[1,3072,512]{2,1,0:T(8,128)} copy(f32[1,3072,512]{2,1,0:T(8,128)S(1)} %bitcast.6) | data formatting | bytes 12582912

commit v3 on v2

--- a/solution.py
+++ b/solution.py
@@ -9,7 +9,8 @@
 
 SIDE = 16
 MEMBERS = 16
-CHUNK = 64
+CHUNK = 96
+PIECE = 4
 WINDOW = 256
 MESH = pl.DeviceIdType.MESH
 STEPS = [(0, 0, 0)] + [
@@ -34,8 +35,8 @@
 
 
 def middle(
-    coef_ref, interp_ref, switch_ref, offsets_ref, out_ref,
-    arrived, leaving, home, weights, whole, matrix, windows, columns,
+    coef_ref, interp_ref, switch_ref, offsets_ref, early_ref, home, matrix,
+    arrived, leaving, weights, whole, windows, columns,
     cosines, sines, cosine_now, sine_now, rotated,
     in_send, in_recv, out_send, out_recv, off_send, off_recv, sw_send, sw_recv, sw_other, weight_sem,
 ):
@@ -136,7 +137,7 @@
     skip = 64 * (me % 2)
 
     def compute(c, carry):
-        pair = columns[pl.ds(pl.multiple_of(skip + c * CHUNK, CHUNK), CHUNK), :]
+        pair = columns[pl.ds(pl.multiple_of(skip + c * CHUNK, 32), CHUNK), :]
         for b in range(MEMBERS):
             phase = pair[:, 2 * b:2 * b + 1] * point_x + pair[:, 2 * b + 1:2 * b + 2] * point_y
             cosine, sine = turn(phase)
@@ -203,10 +204,12 @@
         pltpu.make_async_copy(home.at[:, at(c)], home.at[:, at(c)], out_recv.at[c]).wait()
         state = home[:, at(c), :].reshape(MEMBERS * CHUNK, 2 * rank)
         switched = jnp.dot(state, matrix[...], preferred_element_type=jnp.float32)
-        out_ref[:, at(c), :] = switched.reshape(MEMBERS, CHUNK, 2 * rank)
+        early_ref[:, at(c), :] = switched.reshape(MEMBERS, CHUNK, 2 * rank)
         return carry
 
-    lax.fori_loop(0, chunks, finish, 0)
+    lax.fori_loop(0, chunks - 1, finish, 0)
+    latest = home.at[:, at(chunks - 1)]
+    pltpu.make_async_copy(latest, latest, out_recv.at[chunks - 1]).wait()
 
     others = pl.ds(0, MEMBERS - 1)
     send(coef_ref.at[others], arrived.at[others], in_send, off_recv, member(1)).wait_send()
@@ -214,6 +217,29 @@
     send(windows.at[others], windows.at[others], off_send, off_recv, member(1)).wait_send()
     sent = whole.at[:, pl.ds(0, rows * (parts - 1))]
     send(sent, sent, sw_send, off_recv, member(1)).wait_send()
+
+
+def flush(early_ref, home_ref, matrix_ref, out_ref, late, early_sem, late_sem):
+    done, width = early_ref.shape[1], matrix_ref.shape[-1]
+    early = [
+        pltpu.make_async_copy(
+            early_ref.at[pl.ds(i, PIECE)], out_ref.at[pl.ds(i, PIECE), pl.ds(0, done)], early_sem.at[i // PIECE]
+        )
+        for i in range(0, MEMBERS, PIECE)
+    ]
+    for copy in early:
+        copy.start()
+    copies = []
+    for i in range(0, MEMBERS, PIECE):
+        state = home_ref[i:i + PIECE, done:, :].reshape(PIECE * CHUNK, width)
+        switched = jnp.dot(state, matrix_ref[...], preferred_element_type=jnp.float32)
+        late[i:i + PIECE] = switched.reshape(PIECE, CHUNK, width)
+        copies.append(pltpu.make_async_copy(
+            late.at[pl.ds(i, PIECE)], out_ref.at[pl.ds(i, PIECE), pl.ds(done, CHUNK)], late_sem.at[i // PIECE]
+        ))
+        copies[-1].start()
+    for copy in early + copies:
+        copy.wait()
 
 
 def body(coefficients, interp, switch, grid_offsets):
@@ -227,18 +253,20 @@
     operands = (
         coefficients.reshape(MEMBERS, share, width), interp, switch[0], jnp.swapaxes(grid_offsets[0], 0, 1)
     )
-    switched = pl.pallas_call(
+    early, home, matrix = pl.pallas_call(
         middle,
-        out_shape=pltpu.VMEM((MEMBERS, share, width), f32),
+        out_shape=(
+            pltpu.VMEM((MEMBERS, share - CHUNK, width), f32),
+            pltpu.VMEM((MEMBERS, share, width), bf16),
+            pltpu.VMEM((width, width), bf16),
+        ),
         in_specs=[pl.BlockSpec(memory_space=pl.ANY)] * 4,
-        out_specs=pl.BlockSpec(memory_space=pltpu.VMEM),
+        out_specs=(pl.BlockSpec(memory_space=pltpu.VMEM),) * 3,
         scratch_shapes=[
-            pltpu.VMEM((MEMBERS, share, width), bf16),
             pltpu.VMEM((MEMBERS, share, width), bf16),
             pltpu.VMEM((MEMBERS, share, width), bf16),
             pltpu.VMEM((levels, 2, 2 * width, width), bf16),
             pltpu.VMEM((2, rank, rank), bf16),
-            pltpu.VMEM((width, width), bf16),
             pltpu.VMEM((MEMBERS, 2, WINDOW), jnp.int32),
             pltpu.VMEM((WINDOW, 2 * MEMBERS), f32),
             pltpu.VMEM((MEMBERS, CHUNK, rank), f32),
@@ -249,10 +277,21 @@
             dma, dma((chunks,)), dma, dma((chunks,)), dma, dma, dma, dma, dma, dma((12 * levels,)),
         ],
         compiler_params=pltpu.CompilerParams(
-            collective_id=0, has_side_effects=True, vmem_limit_bytes=48 << 20
+            collective_id=0, has_side_effects=True, vmem_limit_bytes=50 << 20
         ),
         name="middle",
     )(*[pltpu.with_memory_space_constraint(operand, pltpu.HBM) for operand in operands])
+    switched = pl.pallas_call(
+        flush,
+        out_shape=jax.ShapeDtypeStruct((MEMBERS, share, width), f32),
+        in_specs=[pl.BlockSpec(memory_space=pltpu.VMEM)] * 3,
+        out_specs=pl.BlockSpec(memory_space=pl.ANY),
+        scratch_shapes=[
+            pltpu.VMEM((MEMBERS, CHUNK, width), f32), dma((MEMBERS // PIECE,)), dma((MEMBERS // PIECE,))
+        ],
+        compiler_params=pltpu.CompilerParams(vmem_limit_bytes=16 << 20),
+        name="flush",
+    )(*[pltpu.with_memory_space_constraint(operand, pltpu.VMEM) for operand in (early, home, matrix)])
     return switched.reshape(1, rows, width)
 
 

time: 157 us -> 156 us (level)
  local copies, waits for them, and re-layouts: 2.71 us -> 0 us
  Pallas kernels: 154 us -> 156 us
    unnamed x1 -> x0, local copies, waits for them, and re-layouts: 2.71 us -> none
    pallas_call x1 -> x2, Pallas kernels: 154 us -> 156 us  [the longest x1 153 us: body(): pl.pallas_call(middle, out_shape=(pltpu.VMEM((MEMBERS, share - CHUNK, wid...]
where the time goes in v3:
time: 156 us
  Pallas kernels  156 us (100%)
    pallas_call x1, Pallas kernels, body(): pl.pallas_call(middle, out_shape=(pltpu.VMEM((MEMBERS, share - CHUNK, wid...  153 us

profile of v3, /device:TPU:33, one launch (start us, length us, event | category | flops | bytes accessed | tf_op | source)
XLA Modules:
  0.0 155.6 jit_solution(11469990316402678050)
XLA Ops:
  0.0 152.8 %middle.1 = (f32[16,96,512]{2,1,0:T(8,128)S(1)}, bf16[16,192,512]{2,1,0:T(8,128)(2,1)S(1)}, bf16[512,512]{1,0:T(8,128)(2,1)S(1)}) custom-call(bf16[16,192,512]{2,1,0:T(8,128)(2,1)} %bitcast.6, bf16[4,2,2,2,256,256]{5,4,3,2,1,0:T(8,128)(2,1)} %interp_ref.1, bf16[2,32,256]{2,1,0:T(8,128)(2,1)} %bitcast.7, s32[2,3072]{1,0:T(2,128)} %bitcast.8), custom_call_target="tpu_custom_call" | custom-call | tf_op jit(solution)/shard_map/middle/pallas_call | solution.py:256
  152.8 2.8 %flush.1 = f32[16,192,512]{2,1,0:T(8,128)} custom-call(f32[16,96,512]{2,1,0:T(8,128)S(1)} %get-tuple-element.8.early_ref, bf16[16,192,512]{2,1,0:T(8,128)(2,1)S(1)} %get-tuple-element.9.home_ref, bf16[512,512]{1,0:T(8,128)(2,1)S(1)} %get-tuple-element.10.matrix_ref), custom_call_target="tpu_custom_call" | custom-call | tf_op jit(solution)/shard_map/flush/pallas_call | solution.py:284

commit v4 on v3

--- a/solution.py
+++ b/solution.py
@@ -10,7 +10,7 @@
 SIDE = 16
 MEMBERS = 16
 CHUNK = 96
-PIECE = 4
+PIECE = 2
 WINDOW = 256
 MESH = pl.DeviceIdType.MESH
 STEPS = [(0, 0, 0)] + [
@@ -35,7 +35,7 @@
 
 
 def middle(
-    coef_ref, interp_ref, switch_ref, offsets_ref, early_ref, home, matrix,
+    coef_ref, interp_ref, switch_ref, offsets_ref, home, matrix,
     arrived, leaving, weights, whole, windows, columns,
     cosines, sines, cosine_now, sine_now, rotated,
     in_send, in_recv, out_send, out_recv, off_send, off_recv, sw_send, sw_recv, sw_other, weight_sem,
@@ -200,16 +200,8 @@
     matrix[rank:, :rank] = -whole[1]
     matrix[rank:, rank:] = whole[0]
 
-    def finish(c, carry):
+    for c in range(chunks):
         pltpu.make_async_copy(home.at[:, at(c)], home.at[:, at(c)], out_recv.at[c]).wait()
-        state = home[:, at(c), :].reshape(MEMBERS * CHUNK, 2 * rank)
-        switched = jnp.dot(state, matrix[...], preferred_element_type=jnp.float32)
-        early_ref[:, at(c), :] = switched.reshape(MEMBERS, CHUNK, 2 * rank)
-        return carry
-
-    lax.fori_loop(0, chunks - 1, finish, 0)
-    latest = home.at[:, at(chunks - 1)]
-    pltpu.make_async_copy(latest, latest, out_recv.at[chunks - 1]).wait()
 
     others = pl.ds(0, MEMBERS - 1)
     send(coef_ref.at[others], arrived.at[others], in_send, off_recv, member(1)).wait_send()
@@ -219,26 +211,18 @@
     send(sent, sent, sw_send, off_recv, member(1)).wait_send()
 
 
-def flush(early_ref, home_ref, matrix_ref, out_ref, late, early_sem, late_sem):
-    done, width = early_ref.shape[1], matrix_ref.shape[-1]
-    early = [
-        pltpu.make_async_copy(
-            early_ref.at[pl.ds(i, PIECE)], out_ref.at[pl.ds(i, PIECE), pl.ds(0, done)], early_sem.at[i // PIECE]
-        )
-        for i in range(0, MEMBERS, PIECE)
-    ]
-    for copy in early:
-        copy.start()
+def flush(home_ref, matrix_ref, out_ref, result, sems):
+    _, share, width = home_ref.shape
     copies = []
     for i in range(0, MEMBERS, PIECE):
-        state = home_ref[i:i + PIECE, done:, :].reshape(PIECE * CHUNK, width)
+        state = home_ref[i:i + PIECE].reshape(PIECE * share, width)
         switched = jnp.dot(state, matrix_ref[...], preferred_element_type=jnp.float32)
-        late[i:i + PIECE] = switched.reshape(PIECE, CHUNK, width)
+        result[i:i + PIECE] = switched.reshape(PIECE, share, width)
         copies.append(pltpu.make_async_copy(
-            late.at[pl.ds(i, PIECE)], out_ref.at[pl.ds(i, PIECE), pl.ds(done, CHUNK)], late_sem.at[i // PIECE]
+            result.at[pl.ds(i, PIECE)], out_ref.at[pl.ds(i, PIECE)], sems.at[i // PIECE]
         ))
         copies[-1].start()
-    for copy in early + copies:
+    for copy in copies:
         copy.wait()
 
 
@@ -253,15 +237,14 @@
     operands = (
         coefficients.reshape(MEMBERS, share, width), interp, switch[0], jnp.swapaxes(grid_offsets[0], 0, 1)
     )
-    early, home, matrix = pl.pallas_call(
+    home, matrix = pl.pallas_call(
         middle,
         out_shape=(
-            pltpu.VMEM((MEMBERS, share - CHUNK, width), f32),
             pltpu.VMEM((MEMBERS, share, width), bf16),
             pltpu.VMEM((width, width), bf16),
         ),
         in_specs=[pl.BlockSpec(memory_space=pl.ANY)] * 4,
-        out_specs=(pl.BlockSpec(memory_space=pltpu.VMEM),) * 3,
+        out_specs=(pl.BlockSpec(memory_space=pltpu.VMEM),) * 2,
         scratch_shapes=[
             pltpu.VMEM((MEMBERS, share, width), bf16),
             pltpu.VMEM((MEMBERS, share, width), bf16),
@@ -284,14 +267,14 @@
     switched = pl.pallas_call(
         flush,
         out_shape=jax.ShapeDtypeStruct((MEMBERS, share, width), f32),
-        in_specs=[pl.BlockSpec(memory_space=pltpu.VMEM)] * 3,
+        in_specs=[pl.BlockSpec(memory_space=pltpu.VMEM)] * 2,
         out_specs=pl.BlockSpec(memory_space=pl.ANY),
         scratch_shapes=[
-            pltpu.VMEM((MEMBERS, CHUNK, width), f32), dma((MEMBERS // PIECE,)), dma((MEMBERS // PIECE,))
+            pltpu.VMEM((MEMBERS, share, width), f32), dma((MEMBERS // PIECE,))
         ],
         compiler_params=pltpu.CompilerParams(vmem_limit_bytes=16 << 20),
         name="flush",
-    )(*[pltpu.with_memory_space_constraint(operand, pltpu.VMEM) for operand in (early, home, matrix)])
+    )(*[pltpu.with_memory_space_constraint(operand, pltpu.VMEM) for operand in (home, matrix)])
     return switched.reshape(1, rows, width)
 
 

time: 156 us -> 155 us (level)
  no operation moved by 1% of the time
where the time goes in v4:
time: 155 us
  Pallas kernels  155 us (100%)
    pallas_call x1, Pallas kernels, body(): pl.pallas_call(middle, out_shape=(pltpu.VMEM((MEMBERS, share, width), bf1...  152 us
    pallas_call x1, Pallas kernels, body(): pl.pallas_call(flush, out_shape=jax.ShapeDtypeStruct((MEMBERS, share, wid...  3.11 us

profile of v4, /device:TPU:33, one launch (start us, length us, event | category | flops | bytes accessed | tf_op | source)
XLA Modules:
  0.0 154.9 jit_solution(4740701992187392422)
XLA Ops:
  0.0 151.8 %middle.1 = (bf16[16,192,512]{2,1,0:T(8,128)(2,1)S(1)}, bf16[512,512]{1,0:T(8,128)(2,1)S(1)}) custom-call(bf16[16,192,512]{2,1,0:T(8,128)(2,1)} %bitcast.6, bf16[4,2,2,2,256,256]{5,4,3,2,1,0:T(8,128)(2,1)} %interp_ref.1, bf16[2,32,256]{2,1,0:T(8,128)(2,1)} %bitcast.7, s32[2,3072]{1,0:T(2,128)} %bitcast.8), custom_call_target="tpu_custom_call" | custom-call | tf_op jit(solution)/shard_map/middle/pallas_call | solution.py:240
  151.8 3.1 %flush.1 = f32[16,192,512]{2,1,0:T(8,128)} custom-call(bf16[16,192,512]{2,1,0:T(8,128)(2,1)S(1)} %get-tuple-element.7.home_ref, bf16[512,512]{1,0:T(8,128)(2,1)S(1)} %get-tuple-element.8.matrix_ref), custom_call_target="tpu_custom_call" | custom-call | tf_op jit(solution)/shard_map/flush/pallas_call | solution.py:267

commit v5 on v4

--- a/solution.py
+++ b/solution.py
@@ -14,7 +14,7 @@
 WINDOW = 256
 MESH = pl.DeviceIdType.MESH
 STEPS = [(0, 0, 0)] + [
-    (y, x, z) for x, y in ((0, 0), (1, 0), (2, 0), (3, 0), (0, 1), (1, 1), (2, 1), (3, 1)) for z in (1, 0) if x + y + z
+    (y, x, z) for x, y in ((2, 1), (1, 1), (3, 1), (2, 0), (1, 0), (3, 0), (0, 1), (0, 0)) for z in (1, 0) if x + y + z
 ]
 
 

time: 155 us -> 155 us (level)
  no operation moved by 1% of the time
where the time goes in v5:
time: 155 us
  Pallas kernels  155 us (100%)
    pallas_call x1, Pallas kernels, body(): pl.pallas_call(middle, out_shape=(pltpu.VMEM((MEMBERS, share, width), bf1...  152 us
    pallas_call x1, Pallas kernels, body(): pl.pallas_call(flush, out_shape=jax.ShapeDtypeStruct((MEMBERS, share, wid...  3.11 us

profile of v5, /device:TPU:33, one launch (start us, length us, event | category | flops | bytes accessed | tf_op | source)
XLA Modules:
  0.0 154.9 jit_solution(12781579421144887021)
XLA Ops:
  0.0 151.8 %middle.1 = (bf16[16,192,512]{2,1,0:T(8,128)(2,1)S(1)}, bf16[512,512]{1,0:T(8,128)(2,1)S(1)}) custom-call(bf16[16,192,512]{2,1,0:T(8,128)(2,1)} %bitcast.6, bf16[4,2,2,2,256,256]{5,4,3,2,1,0:T(8,128)(2,1)} %interp_ref.1, bf16[2,32,256]{2,1,0:T(8,128)(2,1)} %bitcast.7, s32[2,3072]{1,0:T(2,128)} %bitcast.8), custom_call_target="tpu_custom_call" | custom-call | tf_op jit(solution)/shard_map/middle/pallas_call | solution.py:240
  151.8 3.1 %flush.1 = f32[16,192,512]{2,1,0:T(8,128)} custom-call(bf16[16,192,512]{2,1,0:T(8,128)(2,1)S(1)} %get-tuple-element.7.home_ref, bf16[512,512]{1,0:T(8,128)(2,1)S(1)} %get-tuple-element.8.matrix_ref), custom_call_target="tpu_custom_call" | custom-call | tf_op jit(solution)/shard_map/flush/pallas_call | solution.py:267
